TPU v7x, 128 devices: a whole 4x4x4 slice. The times are simulated.
128 devices in a mesh: dp: 4 (over x_hi, core), tensor: 32 (over x_lo, y, z).
Axes of the slice: x: 4 (x_hi: 2, x_lo: 2; x = x_hi * 2 + x_lo), y: 4, z: 4, core: 2. Of those that a mesh axis runs over, the one named last changes fastest.
Arguments:
- teacher_hidden: bfloat16 [5120, 24576], P('dp', 'tensor'), may hold values from -40 to 40, as said below
- teacher_down: bfloat16 [24576, 3072], P('tensor'), may hold values from -0.0390625 to 0.0390625
- teacher_gain: float32 [3072], replicated, may hold values from 0.5 to 1.5
- student_stream: bfloat16 [5120, 1024], P(('dp', 'tensor')), may hold values from -45 to 45
- contexts: bfloat16 [2, 5120, 1024], P(None, ('dp', 'tensor')), may hold values from -6 to 6
- proj_weight: bfloat16 [2, 1024, 1024], P(None, 'tensor'), may hold values from -0.1875 to 0.1875
- student_gain: float32 [1024], replicated, may hold values from 0.5 to 1.5
- head_weight: bfloat16 [1024, 3072], P(None, 'tensor'), may hold values from -0.1875 to 0.1875
Outputs:
- head_grad: float32 [1024, 3072], P(None, 'tensor')
- proj_grad: float32 [2, 1024, 1024], P(None, 'tensor')
Inputs may be any that keep to these rules, and one draw needn't show every extreme that they name: `teacher_hidden`: teacher activations of every row.
All inputs are finite; a program needn't handle non-finite values.
Results may differ from a plain program's by a relative error of at most 0.0085.
Values may be sent and summed in bfloat16 or wider, within the bound.
A program may use at most 128 MiB of HBM per device.

v0:
```python
import math

import jax
import jax.numpy as jnp
from jax import lax
from jax.sharding import PartitionSpec as P

epsilon = 1e-06


def normalize(values, gain):
    mean_value = jnp.mean(values, axis=-1, keepdims=True)
    centered = values - mean_value
    variance = jnp.mean(centered * centered, axis=-1, keepdims=True)
    inv_std = lax.rsqrt(variance + epsilon)
    normed = centered * inv_std
    return (normed * gain, normed, inv_std)


def normalize_back(grad_out, gain, normed, inv_std):
    weighted = grad_out * gain
    first_mean = jnp.mean(weighted, axis=-1, keepdims=True)
    second_mean = jnp.mean(weighted * normed, axis=-1, keepdims=True)
    return inv_std * (weighted - first_mean - normed * second_mean)


def per_device(
    teacher_hidden,
    teacher_down,
    teacher_gain,
    student_stream,
    contexts,
    proj_weight,
    student_gain,
    head_weight,
):
    member = lax.axis_index("tensor")
    own_rows = student_stream.shape[0]
    group_rows = teacher_hidden.shape[0]
    factor = 1.0 / math.sqrt(group_rows * lax.axis_size("dp"))
    summed = lax.psum(
        jnp.dot(teacher_hidden, teacher_down, preferred_element_type=jnp.float32), "tensor"
    )
    target_all = normalize(summed, teacher_gain)[0].astype(jnp.bfloat16)
    target_rows = lax.dynamic_slice_in_dim(target_all, member * own_rows, own_rows, 0)
    gathered_proj = lax.all_gather(proj_weight, "tensor", axis=1, tiled=True)
    stream = student_stream.astype(jnp.float32) + jnp.einsum(
        "lrc,lcd->rd", contexts, gathered_proj, preferred_element_type=jnp.float32
    )
    scaled, normed, inv_std = normalize(stream, student_gain)
    features = scaled.astype(jnp.bfloat16)
    whole_head = lax.all_gather(head_weight, "tensor", axis=1, tiled=True)
    predicted = jnp.dot(features, whole_head, preferred_element_type=jnp.float32)
    pred_grad = ((predicted - target_rows.astype(jnp.float32)) * factor).astype(jnp.bfloat16)
    head_term = lax.dot_general(
        features, pred_grad, (((0,), (0,)), ((), ())), preferred_element_type=jnp.float32
    )
    head_part = lax.psum_scatter(head_term, "tensor", scatter_dimension=1, tiled=True)
    feature_grad = lax.dot_general(
        pred_grad, whole_head, (((1,), (1,)), ((), ())), preferred_element_type=jnp.float32
    )
    stream_grad = normalize_back(feature_grad, student_gain, normed, inv_std).astype(jnp.bfloat16)
    proj_term = jnp.einsum("lrc,rd->lcd", contexts, stream_grad, preferred_element_type=jnp.float32)
    proj_part = lax.psum_scatter(proj_term, "tensor", scatter_dimension=1, tiled=True)
    head_grad, proj_grad = lax.psum((head_part, proj_part), "dp")
    return (head_grad, proj_grad)


def solution(mesh):
    in_specs = (
        P("dp", "tensor"),
        P("tensor", None),
        P(),
        P(("dp", "tensor"), None),
        P(None, ("dp", "tensor"), None),
        P(None, "tensor", None),
        P(),
        P(None, "tensor"),
    )
    out_specs = (P(None, "tensor"), P(None, "tensor", None))
    return jax.shard_map(
        per_device, mesh=mesh, in_specs=in_specs, out_specs=out_specs, check_vma=False
    )
```

profile of v0, /device:TPU:1, one launch (start us, length us, event | category | flops | bytes accessed | tf_op | source)
XLA Modules:
  0.0 1336.0 jit_solution(11113065769948116327)
XLA Ops:
  7.2 0.0 copy-start
  7.2 0.0 all-gather.3.cloned.1.call-start
  7.2 0.7 all-gather.3.cloned.1.call-update
  7.9 0.0 all-reduce.6.cloned.1.call-start
  8.0 0.8 copy-done
  8.7 11.9 fusion.14
  20.7 0.0 copy-start.3
  20.7 0.0 copy-start.5
  20.7 0.0 all-reduce.6.cloned.1.call-update
  20.7 0.0 all-gather.5.cloned.1.call-start
  20.7 0.7 all-gather.5.cloned.1.call-update
  21.4 0.0 all-reduce.8.cloned.1.call-start
  21.5 129.5 %all-gather.3.cloned.1.call-done = bf16[2,1024,1024]{2,1,0:T(8,128)(2,1)} async-done(((bf16[2,32,1024]{2,1,0:T(8,128)(2,1)}), bf16[2,1024,1024]{2,1,0:T(8,128)(2,1)}) %all-gather.3.cloned.1.call-update) | async-done | bytes 4194320 | tf_op jit(solution)/shard_map/all_gather | solution.py:46
  151.0 0.0 copy-done.3
  151.0 0.0 copy-done.5
  151.0 3.1 fusion.13
  154.1 0.2 multiply_reduce_fusion.2
  154.3 391.3 %all-reduce.6.cloned.1.call-done = f32[1280,3072]{1,0:T(8,128)} async-done(((f32[1280,3072]{1,0:T(8,128)}), f32[1280,3072]{1,0:T(8,128)}) %all-reduce.6.cloned.1.call-update) | async-done | bytes 15728656 | tf_op jit(solution)/shard_map/psum | solution.py:41
  545.6 6.2 reduce_sum.56
  551.8 0.0 copy-start.4
  551.9 0.0 copy-start.6
  551.9 11.6 multiply_reduce_fusion
  563.5 0.1 dynamic-slice.2
  563.5 139.4 %all-gather.5.cloned.1.call-done = bf16[1024,3072]{0,1:T(8,128)(2,1)} async-done(((bf16[1024,96]{0,1:T(8,128)(2,1)}), bf16[1024,3072]{0,1:T(8,128)(2,1)}) %all-gather.5.cloned.1.call-update) | async-done | bytes 6291472 | tf_op jit(solution)/shard_map/all_gather | solution.py:52
  702.9 0.0 copy-start.2
  702.9 0.0 copy-done.4
  702.9 0.0 copy-done.6
  702.9 5.0 fusion.1
  707.9 0.0 copy-done.2
  707.9 1.3 fusion.12
  709.2 4.6 convolution_bitcast_fusion
  713.9 13.4 %copy.11 = f32[2,1024,1024]{2,0,1:T(2,128)} copy(f32[2,1024,1024]{1,2,0:T(8,128)} %convolution_bitcast_fusion) | data formatting | bytes 16777216 | tf_op jit(solution)/shard_map/lrc,rd->lcd/dot_general | solution.py:63
  727.2 0.0 all-reduce.8.cloned.1.call-update
  727.3 0.0 reduce-scatter.2.cloned.1.call-start
  727.3 6.4 fusion.11
  733.7 0.0 copy-start.1
  733.7 0.0 copy-start.7
  733.7 0.0 reduce-scatter.2.cloned.1.call-update
  733.8 0.0 all-reduce.10.cloned.1.call-start
  733.8 0.7 copy-done.7
  734.5 0.6 dynamic-slice
  735.8 335.5 %all-reduce.8.cloned.1.call-done = f32[2,1024,1024]{2,0,1:T(2,128)} async-done(((f32[2,1024,1024]{2,0,1:T(2,128)}), f32[2,1024,1024]{2,0,1:T(2,128)}) %all-reduce.8.cloned.1.call-update) | async-done | bytes 8388624
  1071.2 1.7 constant_dynamic-slice_fusion
  1072.9 187.5 %reduce-scatter.2.cloned.1.call-done = f32[1024,96]{0,1:T(8,128)} async-done(((f32[1024,3072]{0,1:T(8,128)}), f32[1024,96]{0,1:T(8,128)}) %reduce-scatter.2.cloned.1.call-update) | async-done | bytes 393232 | tf_op jit(solution)/shard_map/reduce_scatter | solution.py:58
  1260.4 0.0 all-reduce.10.cloned.1.call-update
  1260.4 65.3 %all-reduce.10.cloned.1.call-done = (f32[1024,96]{0,1:T(8,128)}, f32[2,32,1024]{2,0,1:T(2,128)}) async-done(((f32[1024,96]{0,1:T(8,128)}, f32[2,32,1024]{2,0,1:T(2,128)}), (f32[1024,96]{0,1:T(8,128)}, f32[2,32,1024]{2,0,1:T(2,128)})) %all-reduce.10.cloned.1.call-update) | async-done | bytes 655376 | tf_op jit(solution)/shard_map/psum | solution.py:65
  1325.7 1.7 copy.12
  1327.4 1.8 copy.17
  1329.2 0.0 copy-done.1
  (5 shorter events, 0.0 us)
Async XLA Ops:
  7.2 1.6 copy-start
  7.2 143.8 %all-gather.3.cloned.1.call-start = ((), (), s32[]{:S(2)}) async-start(), calls=%async_computation.1 | async-start | bytes 4325376 | tf_op jit(solution)/shard_map/all_gather | solution.py:46
  7.9 537.7 %all-reduce.6.cloned.1.call-start = ((), (), s32[]{:S(2)}) async-start(), calls=%async_computation.3 | async-start | bytes 31457280 | tf_op jit(solution)/shard_map/psum | solution.py:41
  20.7 130.3 %copy-start.3 = (bf16[2,40,1024]{2,1,0:T(8,128)(2,1)S(1)}, bf16[2,40,1024]{2,1,0:T(8,128)(2,1)}, u32[]{:S(2)}) copy-start(bf16[2,40,1024]{2,1,0:T(8,128)(2,1)} %param.12) | copy-start | bytes 491524
  20.7 130.3 %copy-start.5 = (bf16[40,1024]{1,0:T(8,128)(2,1)S(1)}, bf16[40,1024]{1,0:T(8,128)(2,1)}, u32[]{:S(2)}) copy-start(bf16[40,1024]{1,0:T(8,128)(2,1)} %param.11) | copy-start | bytes 245764
  20.7 682.2 %all-gather.5.cloned.1.call-start = ((), (), s32[]{:S(2)}) async-start(), calls=%async_computation.2 | async-start | bytes 6488064 | tf_op jit(solution)/shard_map/all_gather | solution.py:52
  21.4 1049.8 %all-reduce.8.cloned.1.call-start = ((), (), s32[]{:S(2)}) async-start(), calls=%async_computation.5 | async-start | bytes 16777216
  551.8 151.1 %copy-start.4 = (f32[1024]{0:T(1024)S(1)}, f32[1024]{0:T(1024)}, u32[]{:S(2)}) copy-start(f32[1024]{0:T(1024)} %param.14) | copy-start | bytes 12292
  551.9 151.1 %copy-start.6 = (f32[3072]{0:T(1024)S(1)}, f32[3072]{0:T(1024)}, u32[]{:S(2)}) copy-start(f32[3072]{0:T(1024)} %param.10) | copy-start | bytes 36868
  702.9 5.0 copy-start.2
  727.3 533.1 %reduce-scatter.2.cloned.1.call-start = ((), (), s32[]{:S(2)}) async-start(), calls=%async_computation.4 | async-start | bytes 12976128 | tf_op jit(solution)/shard_map/reduce_scatter | solution.py:58
  733.7 595.5 %copy-start.1 = (bf16[1280,768]{1,0:T(8,128)(2,1)S(1)}, bf16[1280,768]{1,0:T(8,128)(2,1)}, u32[]{:S(2)}) copy-start(bf16[1280,768]{1,0:T(8,128)(2,1)} %param.8) | copy-start | bytes 5898244
  733.7 0.8 copy-start.7
  733.8 591.9 %all-reduce.10.cloned.1.call-start = ((), (), s32[]{:S(2)}) async-start(), calls=%async_computation.6 | async-start | bytes 1310720 | tf_op jit(solution)/shard_map/psum | solution.py:65
Sparse Core Ops, SparseCore 0:
  9.7 141.2 all-gather.2
  153.5 392.0 all-reduce.5
  547.2 155.6 all-gather.4
  727.4 343.7 all-reduce.7
  1073.5 186.8 reduce-scatter.1
  1263.4 62.2 all-reduce.9
where the time goes:
time: 1340 us
  waiting for transfers between devices  1250 us (93%)
  matrix products  32.4 us (2%)
  local copies, waits for them, and re-layouts  20.7 us (2%)
  other arithmetic  18.1 us (1%)
  between operations  14.8 us (1%)
    psum x1, waiting for transfers between devices, per_device(): lax.psum(jnp.dot(teacher_hidden, teacher_down, preferred_element_type=jnp...  391 us
    unnamed x7, waiting for transfers between devices  337 us
    reduce_scatter x1, waiting for transfers between devices, per_device(): lax.psum_scatter(head_term, 'tensor', scatter_dimension=1, tiled=True)  187 us
    all_gather x1, waiting for transfers between devices, per_device(): whole_head = lax.all_gather(head_weight, 'tensor', axis=1, tiled=True)  139 us
    all_gather x1, waiting for transfers between devices, per_device(): gathered_proj = lax.all_gather(proj_weight, 'tensor', axis=1, tiled=True)  129 us
    psum x1, waiting for transfers between devices, per_device(): head_grad, proj_grad = lax.psum((head_part, proj_part), 'dp')  65.3 us
  transfers between devices with their start and end apart: 6, of which 6 were waited for; matrix products, arithmetic and copies ran while one was open for 3% of the time, Pallas kernels for 0%

commit v1 on v0

v1 whole, which is shorter than its diff:
```python
import functools
import math

import jax
import jax.numpy as jnp
from jax import lax
from jax.experimental import pallas as pl
from jax.experimental.pallas import tpu as pltpu
from jax.sharding import PartitionSpec as P

MESH = pl.DeviceIdType.MESH
F32 = jnp.float32
BF16 = jnp.bfloat16
EPS = 1e-06
OWN, PAD = 40, 48
SCALE = 1.0 / math.sqrt(5120)


def dot(a, b):
    return jnp.dot(a, b, preferred_element_type=F32)


def dot_nt(a, b):
    return lax.dot_general(a, b, (((1,), (1,)), ((), ())), preferred_element_type=F32)


def dot_tn(a, b):
    return lax.dot_general(a, b, (((0,), (0,)), ((), ())), preferred_element_type=F32)


def kernel(
    hid, down, tgain, stream_in, ctx, pw, sgain, headt,
    hg_out, pg_out,
    hid_v, down_v,
    send1, own1, rly1, land1,
    send2, own2, rly2, land2,
    send3, land3,
    tsum,
    ctx_s, ctx_r, ctx_f,
    wk, hk,
    st_s, st_r, feat_s, feat_r, fwide,
    normed_v, istd_v, pred,
    tpad, stat, rpad, grad,
    fg, fg_s, fg_r, sg_s, sg_r, sgw,
    hx, hcr, hy, hyo, hzr, hz, hxr,
    px, pcr, py, pyo, pzr, pz, pxr,
    hfin, pfin,
    lsem, ssem, rsem,
):
    dp = lax.axis_index("dp")
    t = lax.axis_index("tensor")
    h, c = dp // 2, dp % 2
    xl, y, z = t // 16, (t // 4) % 4, t % 4
    xx = 2 * h + xl

    def dev(h_, c_, xl_, y_, z_):
        return {"dp": h_ * 2 + c_, "tensor": xl_ * 16 + y_ * 4 + z_}

    def dev_y(k):
        return dev(h, c, xl, (y + k) % 4, z)

    def dev_z(k):
        return dev(h, c, xl, y, (z + k) % 4)

    def dev_x(k):
        n = (xx + k) % 4
        return dev(n // 2, c, n % 2, y, z)

    xlo = dev(h, c, 1 - xl, y, z)
    other = dev(h, 1 - c, xl, y, z)

    slots = [0]
    copies = []

    def send(src, dst, to):
        i = slots[0]
        slots[0] += 1
        copy = pltpu.make_async_remote_copy(
            src_ref=src, dst_ref=dst, send_sem=ssem.at[i], recv_sem=rsem.at[i],
            device_id=to, device_id_type=MESH,
        )
        copy.start()
        copies.append(copy)
        return copy

    loads = []

    def load(src, dst):
        copy = pltpu.make_async_copy(src, dst, lsem.at[len(loads)])
        copy.start()
        loads.append(copy)

    load(hid, hid_v)

    def dcol(half, q):
        return down.at[:, pl.ds(pl.multiple_of(1536 * half + 384 * q, 128), 384)]

    load(dcol(0, (y + 2) % 4), down_v.at[0, 2])
    for q in range(4):
        load(dcol(1, q), down_v.at[1, q])
    for k in (1, 3, 0):
        load(dcol(0, (y + k) % 4), down_v.at[0, k])

    barrier = pltpu.get_barrier_semaphore()
    for to in (
        [dev_y(k) for k in (1, 2, 3)] + [dev_z(k) for k in (1, 2, 3)]
        + [dev_x(k) for k in (1, 2, 3)] + [other]
    ):
        pl.semaphore_signal(barrier, 1, device_id=to, device_id_type=MESH)

    fill = jnp.zeros((16, 1024), BF16)
    for buf in (st_s, fg_s):
        for k in range(buf.shape[0]):
            buf[k, 32:48, :] = fill
    feat_s[32:48, :] = fill
    sg_s[32:48, :] = fill
    for k in range(4):
        for j in range(4):
            ctx_s[k, j, 32:48, :] = fill[:, :128]
    tpad[...] = jnp.zeros_like(tpad)
    rpad[...] = jnp.zeros_like(rpad)

    for k in range(4):
        q = (y + k) % 4
        for layer in range(2):
            for half in range(2):
                cols = pl.ds(pl.multiple_of(512 * half + 128 * q, 128), 128)
                ctx_s[k, 2 * layer + half, 0:OWN, :] = ctx[layer, :, cols]
    pl.semaphore_wait(barrier, 10)

    ctx_c = [send(ctx_s.at[k], ctx_r.at[y], dev_y(k)) for k in (2, 1, 3)]
    ctx_r[y] = ctx_s[0]

    lanes = pl.ds(pl.multiple_of(512 * c, 128), 512)
    wz_c = [send(pw.at[:, :, lanes], wk.at[:, xl, z, :, lanes], dev_z(k)) for k in (2, 1, 3)]
    hz_c = [send(headt.at[:, lanes], hk.at[xl, z, :, lanes], dev_z(k)) for k in (2, 1, 3)]
    wk[:, xl, z, :, lanes] = pw[:, :, lanes]
    hk[xl, z, :, lanes] = headt[:, lanes]

    def product(ab, k):
        def tile(i, carry):
            if ab == 0:
                value = dot(hid_v[i], down_v[0, k])
            else:
                value = dot(hid_v[(z + k) % 4], down_v[1, i])
            if k == 0:
                own1[ab, i] = value
            else:
                send1[ab, k - 1, i] = value.astype(BF16)
            return carry

        lax.fori_loop(0, 4, tile, 0)

    def ring(ab, n):
        return dev_y if (ab == 0) == (n == 4) else dev_z

    def relay_out(sbuf, rly, ab, n):
        to = ring(ab, n)
        m = n // 2
        return [
            send(sbuf.at[ab, 1, pl.ds(0, m)], rly.at[ab, 0], to(1)),
            send(sbuf.at[ab, 1, pl.ds(m, m)], rly.at[ab, 1], to(3)),
        ]

    def direct_out(sbuf, land, ab, n, k):
        to = ring(ab, n)
        m = n // 2
        if k == 1:
            return send(sbuf.at[ab, 0, pl.ds(m, m)], land.at[ab, 0, pl.ds(m, m)], to(1))
        return send(sbuf.at[ab, 2, pl.ds(0, m)], land.at[ab, 1, pl.ds(0, m)], to(3))

    def relay_on(sbuf, rly, land, ab, n, arrivals):
        to = ring(ab, n)
        m = n // 2
        out = []
        arrivals[0].wait_recv()
        for i in range(m):
            sbuf[ab, 0, i] = (sbuf[ab, 0, i].astype(F32) + rly[ab, 0, i].astype(F32)).astype(BF16)
        out.append(send(sbuf.at[ab, 0, pl.ds(0, m)], land.at[ab, 0, pl.ds(0, m)], to(1)))
        arrivals[1].wait_recv()
        for i in range(m):
            sbuf[ab, 2, m + i] = (sbuf[ab, 2, m + i].astype(F32) + rly[ab, 1, i].astype(F32)).astype(BF16)
        out.append(send(sbuf.at[ab, 2, pl.ds(m, m)], land.at[ab, 1, pl.ds(m, m)], to(3)))
        return out

    loads[0].wait()
    loads[1].wait()
    product(0, 2)
    r1 = [relay_out(send1, rly1, 0, 4), None]
    for i in range(2, 6):
        loads[i].wait()
    product(1, 2)
    r1[1] = relay_out(send1, rly1, 1, 4)
    d1 = [[], []]
    for i in range(6, 9):
        loads[i].wait()
    product(0, 1)
    d1[0].append(direct_out(send1, land1, 0, 4, 1))
    product(0, 3)
    d1[0].append(direct_out(send1, land1, 0, 4, 3))
    product(1, 1)
    d1[1].append(direct_out(send1, land1, 1, 4, 1))
    product(1, 3)
    d1[1].append(direct_out(send1, land1, 1, 4, 3))

    for w in ctx_c:
        w.wait_recv()
    for q in range(4):
        for j in range(4):
            ctx_f[OWN * q : OWN * q + OWN, 128 * j : 128 * j + 128] = ctx_r[q, j].astype(F32)[0:OWN]
    d1[0] += relay_on(send1, rly1, land1, 0, 4, r1[0])
    d1[1] += relay_on(send1, rly1, land1, 1, 4, r1[1])
    for w in wz_c + hz_c:
        w.wait_recv()
    wx_c = [
        send(wk.at[:, xl, :, :, lanes], wk.at[:, xl, :, :, lanes], xlo),
        send(hk.at[xl, :, :, lanes], hk.at[xl, :, :, lanes], xlo),
    ]
    product(0, 0)
    product(1, 0)
    wx_c[0].wait_recv()
    wc_c = [send(wk.at[:, :, :, :, lanes], wk.at[:, :, :, :, lanes], other)]
    wx_c[1].wait_recv()
    wc_c.append(send(hk.at[:, :, :, lanes], hk.at[:, :, :, lanes], other))
    wc_c[0].wait_recv()
    part = dot(ctx_f[...].astype(BF16), wk[...].reshape(512, 1024))
    fg[...] = part.reshape(4, OWN, 1024)
    for k in (2, 1, 3):
        st_s[k - 1, 0:OWN, :] = fg[(y + k) % 4].astype(BF16)
    st_c = [send(st_s.at[k - 1], st_r.at[k - 1], dev_y(k)) for k in (2, 1, 3)]
    stream = stream_in[...].astype(F32) + fg[y]
    for w in st_c:
        w.wait_recv()
    for k in range(3):
        stream = stream + st_r[k].astype(F32)[0:OWN]
    centered = stream - jnp.mean(stream, axis=-1, keepdims=True)
    istd = lax.rsqrt(jnp.mean(centered * centered, axis=-1, keepdims=True) + EPS)
    normed = centered * istd
    normed_v[...] = normed
    istd_v[...] = jnp.broadcast_to(istd, istd_v.shape)
    feat_s[0:OWN, :] = (normed * sgain[...]).astype(BF16)
    ft_c = [send(feat_s, feat_r.at[y], dev_y(k)) for k in (2, 1, 3)]
    feat_r[y] = feat_s[...]

    for ab in range(2):
        for w in d1[ab]:
            w.wait_recv()

    def total1(ab, k):
        q = ((z if ab == 0 else y) + k) % 4
        value = own1[ab, q] + land1[ab, 0, q].astype(F32) + land1[ab, 1, q].astype(F32)
        if k == 0:
            own2[ab] = value.reshape(2, 160, 384)
        else:
            send2[ab, k - 1] = value.reshape(2, 160, 384).astype(BF16)

    r2, d2 = [None, None], [[], []]
    for ab in range(2):
        total1(ab, 2)
        r2[ab] = relay_out(send2, rly2, ab, 2)
    for ab in range(2):
        for k in (1, 3):
            total1(ab, k)
            d2[ab].append(direct_out(send2, land2, ab, 2, k))
    for ab in range(2):
        total1(ab, 0)
    for ab in range(2):
        d2[ab] += relay_on(send2, rly2, land2, ab, 2, r2[ab])

    for w in ft_c:
        w.wait_recv()
    for q in range(4):
        fwide[OWN * q : OWN * q + OWN, :] = feat_r[q].astype(F32)[0:OWN]
    feats = fwide[...].astype(BF16)
    wc_c[1].wait_recv()
    pred[...] = dot_nt(feats, hk[...].reshape(768, 1024))

    for ab in range(2):
        for w in d2[ab]:
            w.wait_recv()

    def total2(ab, q):
        return own2[ab, q] + land2[ab, 0, q].astype(F32) + land2[ab, 1, q].astype(F32)

    x3 = []
    for ab in range(2):
        send3[ab] = total2(ab, 1 - xl).astype(BF16)
        x3.append(send(send3.at[ab], land3.at[ab], xlo))
    for ab in range(2):
        tsum[:, 384 * ab : 384 * ab + 384] = total2(ab, xl)
    for ab in range(2):
        x3[ab].wait_recv()
        tsum[:, 384 * ab : 384 * ab + 384] += land3[ab].astype(F32)

    teach = tsum[...]
    mean_own = jnp.mean(teach, axis=-1, keepdims=True)
    cent = teach - mean_own
    m2_own = jnp.sum(cent * cent, axis=-1, keepdims=True)
    lane = lax.broadcasted_iota(jnp.int32, (160, 128), 1)
    tpad[0:160, :] = jnp.where(lane == 0, mean_own, jnp.where(lane == 1, m2_own, 0.0))
    stat[0] = tpad[...].T[0:8, :]
    sc = [send(stat.at[0], stat.at[k], dev_y(k)) for k in (2, 1, 3)]
    for w in sc:
        w.wait_recv()
    means = [stat[k, 0:1, :] for k in range(4)]
    mean_row = (means[0] + means[1] + means[2] + means[3]) * 0.25
    m2_row = sum(stat[k, 1:2, :] for k in range(4)) + 768.0 * sum((m - mean_row) ** 2 for m in means)
    rpad[0:1, :] = mean_row
    rpad[1:2, :] = lax.rsqrt(m2_row * (1.0 / 3072) + EPS)
    cols = rpad[...].T
    mean_col, istd_col = cols[0:160, 0:1], cols[0:160, 1:2]
    for half in range(2):
        s = slice(384 * half, 384 * half + 384)
        target = ((tsum[:, s] - mean_col) * istd_col * tgain[half, y]).astype(BF16)
        grad[:, s] = ((pred[:, s] - target.astype(F32)) * SCALE).astype(BF16)

    grads = grad[...]
    fg[...] = dot(grads, hk[...].reshape(768, 1024)).reshape(4, OWN, 1024)
    for k in (2, 1, 3):
        fg_s[k - 1, 0:OWN, :] = fg[(y + k) % 4].astype(BF16)
    fg_c = [send(fg_s.at[k - 1], fg_r.at[k - 1], dev_y(k)) for k in (2, 1, 3)]

    hgt = dot_tn(grads, feats).astype(BF16)
    for half in range(2):
        hx[half] = hgt[:, 512 * half : 512 * half + 512].reshape(2, 4, 96, 512)

    def core_out(xbuf, crbuf):
        return send(xbuf.at[1 - c], crbuf, other)

    def z_out(xbuf, crbuf, ybuf, yown, zrbuf, arrival):
        arrival.wait_recv()
        out = []
        for k in (2, 1, 3, 0):
            q = (z + k) % 4
            value = xbuf[c, :, q].astype(F32) + crbuf[:, q].astype(F32)
            if k == 0:
                yown[...] = value
            else:
                ybuf[k - 1] = value.astype(BF16)
                out.append(send(ybuf.at[k - 1], zrbuf.at[k - 1], dev_z(k)))
        return out

    def x_out(yown, zrbuf, zbuf, xrbuf, arrivals):
        for w in arrivals:
            w.wait_recv()
        value = yown[...] + zrbuf[0].astype(F32) + zrbuf[1].astype(F32) + zrbuf[2].astype(F32)
        zbuf[...] = value.astype(BF16)
        out = [
            send(zbuf.at[1 - xl if k % 2 else xl], xrbuf.at[xx], dev_x(k)) for k in (2, 1, 3)
        ]
        xrbuf[xx] = zbuf[xl]
        return out

    def last(xrbuf, fin, arrivals):
        for w in arrivals:
            w.wait_recv()
        fin[c] = (xrbuf[0].astype(F32) + xrbuf[1].astype(F32)) + (xrbuf[2].astype(F32) + xrbuf[3].astype(F32))
        return send(fin.at[c], fin.at[c], other)

    hc_c = core_out(hx, hcr)

    gsum = fg[y]
    for w in fg_c:
        w.wait_recv()
    for k in range(3):
        gsum = gsum + fg_r[k].astype(F32)[0:OWN]
    weighted = gsum * sgain[...]
    nrm = normed_v[...]
    first = jnp.mean(weighted, axis=-1, keepdims=True)
    second = jnp.mean(weighted * nrm, axis=-1, keepdims=True)
    sg_s[0:OWN, :] = (istd_v[:, 0:1] * (weighted - first - nrm * second)).astype(BF16)
    sg_c = [send(sg_s, sg_r.at[y], dev_y(k)) for k in (2, 1, 3)]
    sg_r[y] = sg_s[...]

    hzc = z_out(hx, hcr, hy, hyo, hzr, hc_c)

    for w in sg_c:
        w.wait_recv()
    for q in range(4):
        sgw[OWN * q : OWN * q + OWN, :] = sg_r[q].astype(F32)[0:OWN]
    sgrads = sgw[...].astype(BF16)
    for layer in range(2):
        for half in range(2):
            j = 2 * layer + half
            block = ctx_f[:, 128 * j : 128 * j + 128].astype(BF16)
            value = dot_tn(block, sgrads).astype(BF16)
            for s in range(2):
                px[s, half, :, layer] = value[:, 512 * s : 512 * s + 512].reshape(4, 32, 512)
    pc_c = core_out(px, pcr)
    hxc = x_out(hyo, hzr, hz, hxr, hzc)
    pzc = z_out(px, pcr, py, pyo, pzr, pc_c)
    hlast = last(hxr, hfin, hxc)
    pxc = x_out(pyo, pzr, pz, pxr, pzc)
    plast = last(pxr, pfin, pxc)
    hlast.wait_recv()
    for s in range(2):
        hg_out[:, 512 * s : 512 * s + 512] = hfin[s]
    plast.wait_recv()
    for s in range(2):
        pg_out[:, :, 512 * s : 512 * s + 512] = pfin[s]
    for copy in copies:
        copy.wait_send()
    assert slots[0] <= N_SLOTS


N_SLOTS = 96


def per_device(
    teacher_hidden, teacher_down, teacher_gain, student_stream, contexts, proj_weight, student_gain, head_weight
):
    hid = teacher_hidden.reshape(2, 4, 4, OWN, 768).transpose(2, 0, 1, 3, 4).reshape(4, 320, 768)
    vmem = pl.BlockSpec(memory_space=pltpu.VMEM)
    hbm = pl.BlockSpec(memory_space=pl.ANY)

    def v(*shape, dtype=BF16):
        return pltpu.VMEM(shape, dtype)

    def reduce_bufs(n, tail):
        return [
            v(2, 2, 4, *tail), v(2, 4, *tail), v(3, 2, *tail), v(2, *tail, dtype=F32),
            v(3, 2, *tail), v(2, *tail), v(4, *tail),
        ]

    scratch = [
        v(4, 320, 768), v(2, 4, 768, 384),
        v(2, 3, 4, 320, 384), v(2, 4, 320, 384, dtype=F32), v(2, 2, 2, 320, 384), v(2, 2, 4, 320, 384),
        v(2, 3, 2, 160, 384), v(2, 2, 160, 384, dtype=F32), v(2, 2, 1, 160, 384), v(2, 2, 2, 160, 384),
        v(2, 160, 384), v(2, 160, 384),
        v(160, 768, dtype=F32),
        v(4, 4, PAD, 128), v(4, 4, PAD, 128), v(160, 512, dtype=F32),
        v(2, 2, 4, 32, 1024), v(2, 4, 96, 1024),
        v(3, PAD, 1024), v(3, PAD, 1024), v(PAD, 1024), v(4, PAD, 1024), v(160, 1024, dtype=F32),
        v(OWN, 1024, dtype=F32), v(OWN, 128, dtype=F32), v(160, 768, dtype=F32),
        v(256, 128, dtype=F32), v(4, 8, 256, dtype=F32), v(128, 256, dtype=F32), v(160, 768),
        v(4, OWN, 1024, dtype=F32), v(3, PAD, 1024), v(3, PAD, 1024), v(PAD, 1024), v(4, PAD, 1024),
        v(160, 1024, dtype=F32),
        *reduce_bufs(96, (96, 512)),
        *reduce_bufs(64, (2, 32, 512)),
        v(2, 96, 512, dtype=F32), v(2, 2, 32, 512, dtype=F32),
        pltpu.SemaphoreType.DMA((16,)), pltpu.SemaphoreType.DMA((N_SLOTS,)), pltpu.SemaphoreType.DMA((N_SLOTS,)),
    ]
    head_grad, proj_grad = pl.pallas_call(
        kernel,
        out_shape=(
            jax.ShapeDtypeStruct((96, 1024), F32),
            jax.ShapeDtypeStruct((2, 32, 1024), F32),
        ),
        in_specs=[hbm, hbm, vmem, vmem, vmem, vmem, vmem, vmem],
        out_specs=(vmem, vmem),
        scratch_shapes=scratch,
        compiler_params=pltpu.CompilerParams(
            collective_id=0, has_side_effects=True, vmem_limit_bytes=56 * 2**20
        ),
        cost_estimate=pl.CostEstimate(flops=6 * 10**9, bytes_accessed=8 * 10**6, transcendentals=0),
    )(
        hid,
        teacher_down,
        teacher_gain.reshape(2, 4, 1, 384),
        student_stream,
        contexts,
        proj_weight,
        student_gain.reshape(1, 1024),
        head_weight.T,
    )
    return head_grad.T, proj_grad


def solution(mesh):
    in_specs = (
        P("dp", "tensor"),
        P("tensor", None),
        P(),
        P(("dp", "tensor"), None),
        P(None, ("dp", "tensor"), None),
        P(None, "tensor", None),
        P(),
        P(None, "tensor"),
    )
    out_specs = (P(None, "tensor"), P(None, "tensor", None))
    return jax.shard_map(
        per_device, mesh=mesh, in_specs=in_specs, out_specs=out_specs, check_vma=False
    )
```

time: 1340 us -> 111 us (0.08)
  waiting for transfers between devices: 1250 us -> 0 us
  Pallas kernels: 0 us -> 104 us
  matrix products: 32.4 us -> 0 us
  other arithmetic: 18.1 us -> 0 us
  local copies, waits for them, and re-layouts: 20.7 us -> 6.41 us
  between operations: 14.8 us -> 0.64 us
    psum x2 -> x0, waiting for transfers between devices: 457 us -> none  [the longest x1 391 us: per_device(): lax.psum(jnp.dot(teacher_hidden, teacher_down, preferred_element_type=jnp...]
    unnamed x7 -> x0, waiting for transfers between devices: 337 us -> none
    all_gather x2 -> x0, waiting for transfers between devices: 269 us -> none  [the longest x1 139 us: per_device(): whole_head = lax.all_gather(head_weight, 'tensor', axis=1, tiled=True)]
    reduce_scatter x1 -> x0, waiting for transfers between devices: 187 us -> none  [per_device(): lax.psum_scatter(head_term, 'tensor', scatter_dimension=1, tiled=True)]
    pallas_call x0 -> x1, Pallas kernels: none -> 104 us  [per_device(): pl.pallas_call(kernel, out_shape=(jax.ShapeDtypeStruct((96, 1024), F32),...]
    dot_general x6 -> x0, matrix products: 32.4 us -> none  [the longest x1 11.9 us: per_device(): jnp.dot(teacher_hidden, teacher_down, preferred_element_type=jnp.float32)]
    reduce_sum x3 -> x0, other arithmetic: 18 us -> none  [the longest x2 11.8 us: normalize(): variance = jnp.mean(centered * centered, axis=-1, keepdims=True)]
  transfers between devices with their start and end apart: 6 -> 0, of which waited for: 6 -> 0; matrix products, arithmetic and copies ran while one was open for 3% -> 0% of each run, Pallas kernels for 0% -> 0%
where the time goes in v1:
time: 111 us
  Pallas kernels  104 us (94%)
  local copies, waits for them, and re-layouts  6.41 us (6%)
    pallas_call x1, Pallas kernels, per_device(): pl.pallas_call(kernel, out_shape=(jax.ShapeDtypeStruct((96, 1024), F32),...  104 us
    unnamed x2, local copies, waits for them, and re-layouts  3.44 us
    reshape x1, local copies, waits for them, and re-layouts, per_device(): teacher_hidden.reshape(2, 4, 4, OWN, 768).transpose(2, 0, 1, 3, 4)  2.98 us

profile of v1, /device:TPU:1, one launch (start us, length us, event | category | flops | bytes accessed | tf_op | source)
XLA Modules:
  0.0 110.6 jit_solution(14229941590223879505)
XLA Ops:
  0.6 3.0 %copy.10 = bf16[2,4,4,40,768]{4,3,1,0,2:T(8,128)(2,1)} copy(bf16[2,4,4,40,768]{4,3,2,1,0:T(8,128)(2,1)} %bitcast.8) | data formatting | bytes 3932160 | tf_op jit(solution)/shard_map/reshape | solution.py:412
  3.6 103.6 %shard_map.95 = (f32[96,1024]{1,0:T(8,128)}, f32[2,32,1024]{2,1,0:T(8,128)}) custom-call(bf16[4,320,768]{2,1,0:T(8,128)(2,1)} %bitcast.9, bf16[768,3072]{1,0:T(8,128)(2,1)} %down.1, f32[2,4,1,384]{3,2,1,0:T(1,128)} %bitcast.12, bf16[40,1024]{1,0:T(8,128)(2,1)} %stream_in.1, bf16[2,40,1024]{2,1,0:T(8,128)(2,1)} %ctx.1, bf16[2,32,1024]{2,1,0:T(8,128)(2,1)} %pw.1, ...), custom_call_target="tpu_custom_call" | custom-call | flops 6000000000 | bytes 8000000 | tf_op jit(solution)/shard_map/pallas_call | solution.py:443
  107.2 1.8 %copy.13 = f32[1024,96]{0,1:T(8,128)} copy(f32[1024,96]{0,1:T(8,128)} %bitcast.10) | data formatting | bytes 786432
  109.0 1.7 %copy.14 = f32[2,32,1024]{2,1,0:T(8,128)} copy(f32[2,32,1024]{2,1,0:T(8,128)} %get-tuple-element.9) | data formatting | bytes 524288

commit v2 on v1

v2 whole, which is shorter than its diff:
```python
import functools
import math

import jax
import jax.numpy as jnp
from jax import lax
from jax.experimental import pallas as pl
from jax.experimental.pallas import tpu as pltpu
from jax.sharding import PartitionSpec as P

MESH = pl.DeviceIdType.MESH
F32 = jnp.float32
BF16 = jnp.bfloat16
EPS = 1e-06
OWN = 40
SIDE = 64
MAIN = 160 - SIDE
SCALE = 1.0 / math.sqrt(5120)


def dot(a, b):
    return jnp.dot(a, b, preferred_element_type=F32)


def dot_nt(a, b):
    return lax.dot_general(a, b, (((1,), (1,)), ((), ())), preferred_element_type=F32)


def pack(v):
    return jnp.concatenate([v[:, 0:512], v[:, 512:1024]], axis=0).astype(BF16)


def unpack(b):
    v = b.astype(F32)
    return jnp.concatenate([v[0:OWN], v[OWN : 2 * OWN]], axis=1)


def dot_tn(a, b):
    return lax.dot_general(a, b, (((0,), (0,)), ((), ())), preferred_element_type=F32)


def kernel(
    hid, down, tgain, stream_in, ctx, pw, sgain, headt,
    hg_out, pg_out,
    hm_v, hs_v, down_v, down_b,
    msend1, mown1, mrly1, mland1, msend2, mown2, mland2,
    ssend1, sown1, srly1, sland1, ssend2, sown2, sland2,
    xs, xr, xown,
    send3, land3,
    tsum,
    strm_s, strm_r, ctx_s, ctx_r, ctx_f,
    wk, hk,
    st_s, st_r, feat_s, feat_r, fwide,
    normed_v, istd_v, pred,
    tpad, stat, rpad, grad,
    fg, fg_s, fg_r, sg_s, sg_r, sgw,
    hx, hcr, hy, hyo, hzr, hz, hxr,
    px0, pcr0, py0, pyo0, pzr0, pz0, pxr0,
    px1, pcr1, py1, pyo1, pzr1, pz1, pxr1,
    hfin, pfin,
    lsem, ssem, rsem, tsem, usem,
):
    dp = lax.axis_index("dp")
    t = lax.axis_index("tensor")
    h, c = dp // 2, dp % 2
    xl, y, z = t // 16, (t // 4) % 4, t % 4
    xx = 2 * h + xl

    def dev(h_, c_, xl_, y_, z_):
        return {"dp": h_ * 2 + c_, "tensor": xl_ * 16 + y_ * 4 + z_}

    def dev_y(k):
        return dev(h, c, xl, (y + k) % 4, z)

    def dev_z(k):
        return dev(h, c, xl, y, (z + k) % 4)

    def dev_x(k):
        n = (xx + k) % 4
        return dev(n // 2, c, n % 2, y, z)

    xlo = dev(h, c, 1 - xl, y, z)
    xhi = dev(1 - h, c, 1 - xl, y, z)
    other = dev(h, 1 - c, xl, y, z)

    slots = [0]
    copies = []

    def send(src, dst, to):
        i = slots[0]
        slots[0] += 1
        copy = pltpu.make_async_remote_copy(
            src_ref=src, dst_ref=dst, send_sem=ssem.at[i], recv_sem=rsem.at[i],
            device_id=to, device_id_type=MESH,
        )
        copy.start()
        copies.append(copy)
        return copy

    loads = []

    def load(src, dst):
        copy = pltpu.make_async_copy(src, dst, lsem.at[len(loads)])
        copy.start()
        loads.append(copy)

    def dcol(q):
        return down.at[:, pl.ds(pl.multiple_of(384 * q, 128), 384)]

    lanes = pl.ds(pl.multiple_of(512 * c, 128), 512)
    for half in range(2):
        load(hid.at[pl.ds(4 * half, 4), pl.ds(0, MAIN)], hm_v.at[:, half])
    load(dcol((y + 2) % 4), down_v.at[2])
    load(down.at[:, pl.ds(1536, 1536)], down_b)
    for half in range(2):
        load(hid.at[pl.ds(4 * half, 4), pl.ds(MAIN, SIDE)], hs_v.at[half])
    load(pw.at[:, :, lanes], wk.at[:, xl, z, :, lanes])
    load(headt.at[:, lanes], hk.at[xl, z, :, lanes])
    for k in (1, 3, 0):
        load(dcol((y + k) % 4), down_v.at[k])

    barrier = pltpu.get_barrier_semaphore()
    for to in (
        [dev_y(k) for k in (1, 2, 3)] + [dev_z(k) for k in (1, 2, 3)]
        + [dev_x(k) for k in (1, 2, 3)] + [other]
    ):
        pl.semaphore_signal(barrier, 1, device_id=to, device_id_type=MESH)
    for j in range(4):
        mine = jnp.where(jnp.logical_and(y == z, z == j), 1, 0)
        to = dev(h, c + mine * (1 - 2 * c), xl, z, j)
        pl.semaphore_signal(barrier, 1, device_id=to, device_id_type=MESH)

    tpad[...] = jnp.zeros_like(tpad)
    rpad[...] = jnp.zeros_like(rpad)

    def main_product(ab, k):
        if ab == 0:
            value = dot(hm_v[...].reshape(8 * MAIN, 768), down_v[k]).reshape(4, 2 * MAIN, 384)
            if k == 0:
                mown1[0] = value
            else:
                msend1[0, k - 1] = value.astype(BF16)
            return

        value = dot(hm_v[(z + k) % 4].reshape(2 * MAIN, 768), down_b[...])
        for i in range(4):
            block = value[:, 384 * i : 384 * i + 384]
            if k == 0:
                mown1[1, i] = block
            else:
                msend1[1, k - 1, i] = block.astype(BF16)

    def side_product_y(k, rows, out):
        out[0, k] = dot(hs_v[rows].reshape(4 * SIDE, 768), down_v[k]).reshape(4, SIDE, 384).astype(out.dtype)

    def side_product_z(rows, out):
        value = dot(hs_v[rows].reshape(4 * SIDE, 768), down_b[...]).reshape(4, SIDE, 1536).astype(out.dtype)
        for q in range(4):
            for i in range(4):
                out[1, (q - z + 4) % 4, i] = value[q, :, 384 * i : 384 * i + 384]

    class Ring:
        def __init__(self, to, ab, n, sbuf, rly, land):
            self.to, self.ab, self.n, self.m = to, ab, n, n // 2
            self.sbuf, self.rly, self.land = sbuf, rly, land
            self.relays, self.final = [], []

        def halves(self):
            return pl.ds(0, self.m), pl.ds(self.m, self.n - self.m)

        def relay_out(self):
            low, high = self.halves()
            for d, part in ((0, low), (1, high)):
                self.relays.append(
                    send(self.sbuf.at[self.ab, 1, part], self.rly.at[self.ab, d, part], self.to(1 + 2 * d))
                )

        def direct_out(self, k):
            low, high = self.halves()
            d, part = (0, high) if k == 1 else (1, low)
            self.final.append(
                send(self.sbuf.at[self.ab, k - 1, part], self.land.at[self.ab, d, part], self.to(k))
            )

        def relay_on(self):
            low, high = self.halves()
            for d, k, part, slabs in (
                (0, 1, low, range(self.m)),
                (1, 3, high, range(self.m, self.n)),
            ):
                self.relays[d].wait_recv()
                for i in slabs:
                    value = self.sbuf[self.ab, k - 1, i].astype(F32) + self.rly[self.ab, d, i].astype(F32)
                    self.sbuf[self.ab, k - 1, i] = value.astype(BF16)
                self.final.append(
                    send(self.sbuf.at[self.ab, k - 1, part], self.land.at[self.ab, d, part], self.to(k))
                )

        def finish(self):
            for w in self.final:
                w.wait_recv()

    main1 = [Ring(dev_y, 0, 4, msend1, mrly1, mland1), Ring(dev_z, 1, 4, msend1, mrly1, mland1)]
    side1 = [Ring(dev_y, 0, 4, ssend1, srly1, sland1), Ring(dev_z, 1, 4, ssend1, srly1, sland1)]

    for i in range(3):
        loads[i].wait()
    main_product(0, 2)
    pl.semaphore_wait(barrier, 14)
    main1[0].relay_out()
    for i in range(3, 6):
        loads[i].wait()
    main_product(1, 2)
    main1[1].relay_out()
    xc = [[None] * 4, [None] * 4]

    def x_first(ab, k):
        xc[ab][k] = send(xs.at[ab, k], xr.at[ab, k], xlo)

    side_product_y(2, 1 - xl, xs)
    x_first(0, 2)

    strm_s[...] = pack(stream_in[...].astype(F32))
    for q in range(4):
        parts = [
            ctx[layer, :, 512 * half + 128 * q : 512 * half + 128 * q + 128].astype(F32)
            for layer in range(2)
            for half in range(2)
        ]
        ctx_s[q] = jnp.concatenate(parts, axis=0).astype(BF16)
    strm_self = jnp.logical_and(y == z, z == y)
    strm_to = pltpu.make_async_remote_copy(
        src_ref=strm_s, dst_ref=strm_r, send_sem=usem.at[8], recv_sem=usem.at[9],
        device_id=dev(h, c, xl, z, y), device_id_type=MESH,
    )

    @pl.when(strm_self)
    def _():
        pltpu.make_async_copy(strm_s, strm_r, usem.at[9]).start()

    @pl.when(jnp.logical_not(strm_self))
    def _():
        strm_to.start()

    ctx_to = []
    for q in range(4):
        mine = jnp.logical_and(y == z, y == q)
        copy = pltpu.make_async_remote_copy(
            src_ref=ctx_s.at[q], dst_ref=ctx_r.at[z], send_sem=usem.at[q], recv_sem=tsem.at[z],
            device_id=dev(h, c, xl, q, y), device_id_type=MESH,
        )
        ctx_to.append((mine, copy))

        @pl.when(mine)
        def _():
            pltpu.make_async_copy(ctx_s.at[q], ctx_r.at[z], tsem.at[z]).start()

        @pl.when(jnp.logical_not(mine))
        def _():
            copy.start()

    loads[6].wait()
    wz_c = [send(wk.at[:, xl, z, :, lanes], wk.at[:, xl, z, :, lanes], dev_z(k)) for k in (2, 1, 3)]
    side_product_z(1 - xl, xs)
    x_first(1, 2)
    for i in range(7, 11):
        loads[i].wait()
    for ab in range(2):
        for k in (1, 3):
            main_product(ab, k)
            main1[ab].direct_out(k)
    for k in (1, 3, 0):
        side_product_y(k, 1 - xl, xs)
        x_first(0, k)
        x_first(1, k)
    main_product(0, 0)
    main_product(1, 0)
    for k in (2, 1, 3, 0):
        side_product_y(k, xl, xown)
    side_product_z(xl, xown)
    for ab in range(2):
        main1[ab].relay_on()
    hz_c = [send(hk.at[xl, z, :, lanes], hk.at[xl, z, :, lanes], dev_z(k)) for k in (2, 1, 3)]

    def side_add(ab, k):
        xc[ab][k].wait_recv()
        value = xown[ab, k] + xr[ab, k].astype(F32)
        if k == 0:
            sown1[ab] = value
        else:
            ssend1[ab, k - 1] = value.astype(BF16)

    for ab in range(2):
        side_add(ab, 2)
        side1[ab].relay_out()
    for w in wz_c:
        w.wait_recv()
    wx_c = [send(wk.at[:, xl, :, :, lanes], wk.at[:, xl, :, :, lanes], xhi)]
    for ab in range(2):
        side_add(ab, 1)
        side1[ab].direct_out(1)

    for j in range(4):
        pltpu.make_async_remote_copy(
            src_ref=ctx_s.at[j], dst_ref=ctx_r.at[j], send_sem=usem.at[j], recv_sem=tsem.at[j],
            device_id=dev(h, c, xl, j, y), device_id_type=MESH,
        ).wait_recv()
        block = ctx_r[j].astype(F32)
        for i in range(4):
            ctx_f[OWN * j : OWN * j + OWN, 128 * i : 128 * i + 128] = block[OWN * i : OWN * i + OWN]
    wx_c[0].wait_recv()
    wc_c = [send(wk.at[:, :, :, :, lanes], wk.at[:, :, :, :, lanes], other)]
    wc_c[0].wait_recv()
    fg[...] = dot(ctx_f[...].astype(BF16), wk[...].reshape(512, 1024)).reshape(4, OWN, 1024)
    for k in (2, 1, 3):
        st_s[k - 1] = pack(fg[(y + k) % 4])
    st_c = [send(st_s.at[k - 1], st_r.at[k - 1], dev_y(k)) for k in (2, 1, 3)]

    def second(part, first, ab):
        own1, land1, own2, send2, land2 = part
        first[ab].finish()
        out = []
        for k in (2, 1, 3, 0):
            q = ((z if ab == 0 else y) + k) % 4
            value = own1[ab, q] + land1[ab, 0, q].astype(F32) + land1[ab, 1, q].astype(F32)
            value = value.reshape(own2.shape[1:])
            if k == 0:
                own2[ab] = value
            else:
                send2[ab, k - 1] = value.astype(BF16)
                to = dev_z(k) if ab == 0 else dev_y(k)
                out.append(send(send2.at[ab, k - 1], land2.at[ab, k - 1], to))
        return out

    main_part = (mown1, mland1, mown2, msend2, mland2)
    side_part = (sown1, sland1, sown2, ssend2, sland2)
    main2, side2 = [None, None], [None, None]
    side_add(0, 3)
    side1[0].direct_out(3)
    side1[0].relay_on()
    main2[0] = second(main_part, main1, 0)
    side_add(1, 3)
    side1[1].direct_out(3)
    side1[1].relay_on()
    main2[1] = second(main_part, main1, 1)
    for w in hz_c:
        w.wait_recv()
    wx_c.append(send(hk.at[xl, :, :, lanes], hk.at[xl, :, :, lanes], xhi))
    strm_to.wait_recv()
    stream = unpack(strm_r[...]) + fg[y]
    for w in st_c:
        w.wait_recv()
    for k in range(3):
        stream = stream + unpack(st_r[k])
    centered = stream - jnp.mean(stream, axis=-1, keepdims=True)
    istd = lax.rsqrt(jnp.mean(centered * centered, axis=-1, keepdims=True) + EPS)
    normed = centered * istd
    normed_v[...] = normed
    istd_v[...] = jnp.broadcast_to(istd, istd_v.shape)
    feat_s[...] = pack(normed * sgain[...])
    ft_c = [send(feat_s, feat_r.at[y], dev_y(k)) for k in (2, 1, 3)]
    feat_r[y] = feat_s[...]
    for ab in range(2):
        side_add(ab, 0)
        side2[ab] = second(side_part, side1, ab)

    def total2(own2, land2, ab, q):
        value = own2[ab, q]
        for k in range(3):
            value = value + land2[ab, k, q].astype(F32)
        return value

    x3 = []
    for ab in range(2):
        for w in main2[ab]:
            w.wait_recv()
        send3[ab] = total2(mown2, mland2, ab, 1 - xl).astype(BF16)
        x3.append(send(send3.at[ab], land3.at[ab], xlo))
    wx_c[1].wait_recv()
    wc_c.append(send(hk.at[:, :, :, lanes], hk.at[:, :, :, lanes], other))

    for w in ft_c:
        w.wait_recv()
    for q in range(4):
        fwide[OWN * q : OWN * q + OWN, :] = unpack(feat_r[q])
    feats = fwide[...].astype(BF16)
    wc_c[1].wait_recv()
    pred[...] = dot_nt(feats, hk[...].reshape(768, 1024))
    for ab in range(2):
        s = slice(384 * ab, 384 * ab + 384)
        for w in side2[ab]:
            w.wait_recv()
        tsum[MAIN:160, s] = total2(sown2, sland2, ab, 0)
        x3[ab].wait_recv()
        tsum[0:MAIN, s] = total2(mown2, mland2, ab, xl) + land3[ab].astype(F32)

    teach = tsum[...]
    mean_own = jnp.mean(teach, axis=-1, keepdims=True)
    cent = teach - mean_own
    m2_own = jnp.sum(cent * cent, axis=-1, keepdims=True)
    lane = lax.broadcasted_iota(jnp.int32, (160, 128), 1)
    tpad[0:160, :] = jnp.where(lane == 0, mean_own, jnp.where(lane == 1, m2_own, 0.0))
    stat[0] = tpad[...].T[0:8, :]
    sc = [send(stat.at[0], stat.at[k], dev_y(k)) for k in (2, 1, 3)]
    for w in sc:
        w.wait_recv()
    means = [stat[k, 0:1, :] for k in range(4)]
    mean_row = (means[0] + means[1] + means[2] + means[3]) * 0.25
    m2_row = sum(stat[k, 1:2, :] for k in range(4)) + 768.0 * sum((m - mean_row) ** 2 for m in means)
    rpad[0:1, :] = mean_row
    rpad[1:2, :] = lax.rsqrt(m2_row * (1.0 / 3072) + EPS)
    cols = rpad[...].T
    mean_col, istd_col = cols[0:160, 0:1], cols[0:160, 1:2]
    for half in range(2):
        s = slice(384 * half, 384 * half + 384)
        target = ((tsum[:, s] - mean_col) * istd_col * tgain[half, y]).astype(BF16)
        grad[:, s] = ((pred[:, s] - target.astype(F32)) * SCALE).astype(BF16)

    grads = grad[...]
    fg[...] = dot(grads, hk[...].reshape(768, 1024)).reshape(4, OWN, 1024)
    for k in (2, 1, 3):
        fg_s[k - 1] = pack(fg[(y + k) % 4])
    fg_c = [send(fg_s.at[k - 1], fg_r.at[k - 1], dev_y(k)) for k in (2, 1, 3)]

    hgt = dot_tn(grads, feats).astype(BF16)
    for half in range(2):
        hx[half] = hgt[:, 512 * half : 512 * half + 512].reshape(2, 4, 96, 512)

    def core_out(xbuf, crbuf):
        return send(xbuf.at[1 - c], crbuf, other)

    def z_out(xbuf, crbuf, ybuf, yown, zrbuf, arrival):
        arrival.wait_recv()
        out = []
        for k in (2, 1, 3, 0):
            q = (z + k) % 4
            value = xbuf[c, :, q].astype(F32) + crbuf[:, q].astype(F32)
            if k == 0:
                yown[...] = value
            else:
                ybuf[k - 1] = value.astype(BF16)
                out.append(send(ybuf.at[k - 1], zrbuf.at[k - 1], dev_z(k)))
        return out

    def x_out(yown, zrbuf, zbuf, xrbuf, arrivals):
        for w in arrivals:
            w.wait_recv()
        value = yown[...] + zrbuf[0].astype(F32) + zrbuf[1].astype(F32) + zrbuf[2].astype(F32)
        zbuf[...] = value.astype(BF16)
        out = [
            send(zbuf.at[1 - xl if k % 2 else xl], xrbuf.at[xx], dev_x(k)) for k in (2, 1, 3)
        ]
        xrbuf[xx] = zbuf[xl]
        return out

    def last(xrbuf, fin, arrivals):
        for w in arrivals:
            w.wait_recv()
        fin[c] = (xrbuf[0].astype(F32) + xrbuf[1].astype(F32)) + (xrbuf[2].astype(F32) + xrbuf[3].astype(F32))
        return send(fin.at[c], fin.at[c], other)

    hc_c = core_out(hx, hcr)

    gsum = fg[y]
    for w in fg_c:
        w.wait_recv()
    for k in range(3):
        gsum = gsum + unpack(fg_r[k])
    weighted = gsum * sgain[...]
    nrm = normed_v[...]
    first = jnp.mean(weighted, axis=-1, keepdims=True)
    second = jnp.mean(weighted * nrm, axis=-1, keepdims=True)
    sg_s[...] = pack(istd_v[:, 0:1] * (weighted - first - nrm * second))
    sg_c = [send(sg_s, sg_r.at[y], dev_y(k)) for k in (2, 1, 3)]
    sg_r[y] = sg_s[...]

    hzc = z_out(hx, hcr, hy, hyo, hzr, hc_c)

    for w in sg_c:
        w.wait_recv()
    for q in range(4):
        sgw[OWN * q : OWN * q + OWN, :] = unpack(sg_r[q])
    sgrads = sgw[...].astype(BF16)
    pbufs = (
        (px0, pcr0, py0, pyo0, pzr0, pz0, pxr0),
        (px1, pcr1, py1, pyo1, pzr1, pz1, pxr1),
    )
    pc_c = []
    for layer in range(2):
        px = pbufs[layer][0]
        for half in range(2):
            j = 2 * layer + half
            block = ctx_f[:, 128 * j : 128 * j + 128].astype(BF16)
            value = dot_tn(block, sgrads).astype(BF16)
            for s in range(2):
                px[s, half] = value[:, 512 * s : 512 * s + 512].reshape(4, 32, 512)
        pc_c.append(core_out(px, pbufs[layer][1]))
    pzc = []
    for layer in range(2):
        px, pcr, py, pyo, pzr, pz, pxr = pbufs[layer]
        pzc.append(z_out(px, pcr, py, pyo, pzr, pc_c[layer]))
    hxc = x_out(hyo, hzr, hz, hxr, hzc)
    pxc = []
    for layer in range(2):
        px, pcr, py, pyo, pzr, pz, pxr = pbufs[layer]
        pxc.append(x_out(pyo, pzr, pz, pxr, pzc[layer]))
    hlast = last(hxr, hfin, hxc)
    plast = [last(pbufs[layer][6], pfin.at[layer], pxc[layer]) for layer in range(2)]
    hlast.wait_recv()
    for s in range(2):
        hg_out[:, 512 * s : 512 * s + 512] = hfin[s]
    for layer in range(2):
        plast[layer].wait_recv()
        for s in range(2):
            pg_out[layer, :, 512 * s : 512 * s + 512] = pfin[layer, s]
    for copy in copies:
        copy.wait_send()

    @pl.when(jnp.logical_not(strm_self))
    def _():
        strm_to.wait_send()

    for mine, copy in ctx_to:

        @pl.when(jnp.logical_not(mine))
        def _():
            copy.wait_send()

    assert slots[0] <= N_SLOTS


N_SLOTS = 128


def emit(hg_in, pg_in, hg_out, pg_out, sem):
    copies = [
        pltpu.make_async_copy(hg_in, hg_out, sem.at[0]),
        pltpu.make_async_copy(pg_in, pg_out, sem.at[1]),
    ]
    for copy in copies:
        copy.start()
    for copy in copies:
        copy.wait()


def per_device(
    teacher_hidden, teacher_down, teacher_gain, student_stream, contexts, proj_weight, student_gain, head_weight
):
    vmem = pl.BlockSpec(memory_space=pltpu.VMEM)
    hbm = pl.BlockSpec(memory_space=pl.ANY)

    def v(*shape, dtype=BF16):
        return pltpu.VMEM(shape, dtype)

    def reduce_bufs(tail):
        return [
            v(2, 2, 4, *tail), v(2, 4, *tail), v(3, 2, *tail), v(2, *tail, dtype=F32),
            v(3, 2, *tail), v(2, *tail), v(4, *tail),
        ]

    def ring_bufs(rows, n, r):
        return [
            v(2, 3, 4, rows, 384), v(2, 4, rows, 384, dtype=F32), v(2, 2, 4, rows, 384), v(2, 2, 4, rows, 384),
            v(2, 3, n, r, 384), v(2, n, r, 384, dtype=F32), v(2, 3, n, r, 384),
        ]

    scratch = [
        v(4, 2, MAIN, 768), v(2, 4, SIDE, 768), v(4, 768, 384), v(768, 1536),
        *ring_bufs(2 * MAIN, 2, MAIN),
        *ring_bufs(SIDE, 1, SIDE),
        v(2, 4, 4, SIDE, 384), v(2, 4, 4, SIDE, 384), v(2, 4, 4, SIDE, 384, dtype=F32),
        v(2, MAIN, 384), v(2, MAIN, 384),
        v(160, 768, dtype=F32),
        v(80, 512), v(80, 512), v(4, 160, 128), v(4, 160, 128), v(160, 512, dtype=F32),
        v(2, 2, 4, 32, 1024), v(2, 4, 96, 1024),
        v(3, 80, 512), v(3, 80, 512), v(80, 512), v(4, 80, 512), v(160, 1024, dtype=F32),
        v(OWN, 1024, dtype=F32), v(OWN, 128, dtype=F32), v(160, 768, dtype=F32),
        v(256, 128, dtype=F32), v(4, 8, 256, dtype=F32), v(128, 256, dtype=F32), v(160, 768),
        v(4, OWN, 1024, dtype=F32), v(3, 80, 512), v(3, 80, 512), v(80, 512), v(4, 80, 512),
        v(160, 1024, dtype=F32),
        *reduce_bufs((96, 512)),
        *reduce_bufs((32, 512)),
        *reduce_bufs((32, 512)),
        v(2, 96, 512, dtype=F32), v(2, 2, 32, 512, dtype=F32),
        pltpu.SemaphoreType.DMA((16,)), pltpu.SemaphoreType.DMA((N_SLOTS,)), pltpu.SemaphoreType.DMA((N_SLOTS,)),
        pltpu.SemaphoreType.DMA((4,)), pltpu.SemaphoreType.DMA((10,)),
    ]
    head_grad, proj_grad = pl.pallas_call(
        kernel,
        out_shape=(
            jax.ShapeDtypeStruct((96, 1024), F32),
            jax.ShapeDtypeStruct((2, 32, 1024), F32),
        ),
        in_specs=[hbm, hbm, vmem, vmem, vmem, hbm, vmem, hbm],
        out_specs=(vmem, vmem),
        scratch_shapes=scratch,
        compiler_params=pltpu.CompilerParams(
            collective_id=0, has_side_effects=True, vmem_limit_bytes=56 * 2**20
        ),
        cost_estimate=pl.CostEstimate(flops=6 * 10**9, bytes_accessed=8 * 10**6, transcendentals=0),
    )(
        teacher_hidden.reshape(8, 160, 768),
        teacher_down,
        teacher_gain.reshape(2, 4, 1, 384),
        student_stream,
        contexts,
        proj_weight,
        student_gain.reshape(1, 1024),
        head_weight.T,
    )
    head_grad, proj_grad = pl.pallas_call(
        emit,
        out_shape=(
            jax.ShapeDtypeStruct((96, 1024), F32),
            jax.ShapeDtypeStruct((2, 32, 1024), F32),
        ),
        in_specs=[vmem, vmem],
        out_specs=(hbm, hbm),
        scratch_shapes=[pltpu.SemaphoreType.DMA((2,))],
    )(head_grad, proj_grad)
    return head_grad.T, proj_grad


def solution(mesh):
    in_specs = (
        P("dp", "tensor"),
        P("tensor", None),
        P(),
        P(("dp", "tensor"), None),
        P(None, ("dp", "tensor"), None),
        P(None, "tensor", None),
        P(),
        P(None, "tensor"),
    )
    out_specs = (P(None, "tensor"), P(None, "tensor", None))
    return jax.shard_map(
        per_device, mesh=mesh, in_specs=in_specs, out_specs=out_specs, check_vma=False
    )
```

time: 111 us -> 95 us (0.86)
  Pallas kernels: 104 us -> 94.2 us
  local copies, waits for them, and re-layouts: 6.41 us -> 0 us
    pallas_call x1, Pallas kernels: 104 us -> 92.3 us  [per_device(): pl.pallas_call(kernel, out_shape=(jax.ShapeDtypeStruct((96, 1024), F32),...]
    unnamed x2 -> x0, local copies, waits for them, and re-layouts: 3.44 us -> none
    reshape x1 -> x0, local copies, waits for them, and re-layouts: 2.98 us -> none  [per_device(): teacher_hidden.reshape(2, 4, 4, OWN, 768).transpose(2, 0, 1, 3, 4)]
    pallas_call x0 -> x1, Pallas kernels: none -> 1.92 us  [per_device(): pl.pallas_call(emit, out_shape=(jax.ShapeDtypeStruct((96, 1024), F32), ja...]
where the time goes in v2:
time: 95 us; the launch traced here: 94.8 us
  Pallas kernels  94.2 us (99%)
    pallas_call x1, Pallas kernels, per_device(): pl.pallas_call(kernel, out_shape=(jax.ShapeDtypeStruct((96, 1024), F32),...  92.3 us
    pallas_call x1, Pallas kernels, per_device(): pl.pallas_call(emit, out_shape=(jax.ShapeDtypeStruct((96, 1024), F32), ja...  1.92 us

profile of v2, /device:TPU:1, one launch (start us, length us, event | category | flops | bytes accessed | tf_op | source)
XLA Modules:
  0.0 94.8 jit_solution(11085540639892502622)
XLA Ops:
  0.6 92.3 %shard_map.95 = (f32[96,1024]{1,0:T(8,128)}, f32[2,32,1024]{2,1,0:T(8,128)}) custom-call(bf16[8,160,768]{2,1,0:T(8,128)(2,1)} %bitcast.5, bf16[768,3072]{1,0:T(8,128)(2,1)} %down.1, f32[2,4,1,384]{3,2,1,0:T(1,128)} %bitcast.8, bf16[40,1024]{1,0:T(8,128)(2,1)} %stream_in.1, bf16[2,40,1024]{2,1,0:T(8,128)(2,1)} %ctx.1, bf16[2,32,1024]{2,1,0:T(8,128)(2,1)} %pw.1, ...), custom_call_target="tpu_custom_call" | custom-call | flops 6000000000 | bytes 8000000 | tf_op jit(solution)/shard_map/pallas_call | solution.py:588
  92.9 1.9 %shard_map.96 = (f32[96,1024]{1,0:T(8,128)}, f32[2,32,1024]{2,1,0:T(8,128)}) custom-call(f32[96,1024]{1,0:T(8,128)} %get-tuple-element.6.hg_in, f32[2,32,1024]{2,1,0:T(8,128)} %get-tuple-element.7.pg_in), custom_call_target="tpu_custom_call" | custom-call | tf_op jit(solution)/shard_map/pallas_call | solution.py:611

commit v3 on v2

--- a/solution.py
+++ b/solution.py
@@ -43,7 +43,7 @@
     hid, down, tgain, stream_in, ctx, pw, sgain, headt,
     hg_out, pg_out,
     hm_v, hs_v, down_v, down_b,
-    msend1, mown1, mrly1, mland1, msend2, mown2, mland2,
+    msend1, mown1, mrly1, mland1, msend2, mown2, mrly2, mland2,
     ssend1, sown1, srly1, sland1, ssend2, sown2, sland2,
     xs, xr, xown,
     send3, land3,
@@ -201,6 +201,7 @@
                 w.wait_recv()
 
     main1 = [Ring(dev_y, 0, 4, msend1, mrly1, mland1), Ring(dev_z, 1, 4, msend1, mrly1, mland1)]
+    main2 = [Ring(dev_z, 0, 2, msend2, mrly2, mland2), Ring(dev_y, 1, 2, msend2, mrly2, mland2)]
     side1 = [Ring(dev_y, 0, 4, ssend1, srly1, sland1), Ring(dev_z, 1, 4, ssend1, srly1, sland1)]
 
     for i in range(3):
@@ -316,36 +317,61 @@
         st_s[k - 1] = pack(fg[(y + k) % 4])
     st_c = [send(st_s.at[k - 1], st_r.at[k - 1], dev_y(k)) for k in (2, 1, 3)]
 
-    def second(part, first, ab):
-        own1, land1, own2, send2, land2 = part
-        first[ab].finish()
+    def total1(own1, land1, ab, k):
+        q = ((z if ab == 0 else y) + k) % 4
+        return own1[ab, q] + land1[ab, 0, q].astype(F32) + land1[ab, 1, q].astype(F32)
+
+    def main_second(ab):
+        main1[ab].finish()
+        for k in (2, 1, 3, 0):
+            value = total1(mown1, mland1, ab, k).reshape(2, MAIN, 384)
+            if k == 0:
+                mown2[ab] = value
+                continue
+            msend2[ab, k - 1] = value.astype(BF16)
+            if k == 2:
+                main2[ab].relay_out()
+            else:
+                main2[ab].direct_out(k)
+
+    def side_second(ab):
+        side1[ab].finish()
         out = []
         for k in (2, 1, 3, 0):
-            q = ((z if ab == 0 else y) + k) % 4
-            value = own1[ab, q] + land1[ab, 0, q].astype(F32) + land1[ab, 1, q].astype(F32)
-            value = value.reshape(own2.shape[1:])
+            value = total1(sown1, sland1, ab, k)
             if k == 0:
-                own2[ab] = value
-            else:
-                send2[ab, k - 1] = value.astype(BF16)
-                to = dev_z(k) if ab == 0 else dev_y(k)
-                out.append(send(send2.at[ab, k - 1], land2.at[ab, k - 1], to))
+                sown2[ab] = value
+                continue
+            ssend2[ab, k - 1] = value.astype(BF16)
+            to = dev_z(k) if ab == 0 else dev_y(k)
+            out.append(send(ssend2.at[ab, k - 1], sland2.at[ab, k - 1], to))
         return out
 
-    main_part = (mown1, mland1, mown2, msend2, mland2)
-    side_part = (sown1, sland1, sown2, ssend2, sland2)
-    main2, side2 = [None, None], [None, None]
     side_add(0, 3)
     side1[0].direct_out(3)
     side1[0].relay_on()
-    main2[0] = second(main_part, main1, 0)
+    main_second(0)
     side_add(1, 3)
     side1[1].direct_out(3)
     side1[1].relay_on()
-    main2[1] = second(main_part, main1, 1)
+    main_second(1)
     for w in hz_c:
         w.wait_recv()
     wx_c.append(send(hk.at[xl, :, :, lanes], hk.at[xl, :, :, lanes], xhi))
+    main2[0].relay_on()
+    main2[1].relay_on()
+    side2 = []
+    for ab in range(2):
+        side_add(ab, 0)
+        side2.append(side_second(ab))
+    def main_total(ab, q):
+        return mown2[ab, q] + mland2[ab, 0, q].astype(F32) + mland2[ab, 1, q].astype(F32)
+
+    x3 = []
+    for ab in range(2):
+        main2[ab].finish()
+        send3[ab] = main_total(ab, 1 - xl).astype(BF16)
+        x3.append(send(send3.at[ab], land3.at[ab], xlo))
     strm_to.wait_recv()
     stream = unpack(strm_r[...]) + fg[y]
     for w in st_c:
@@ -360,39 +386,20 @@
     feat_s[...] = pack(normed * sgain[...])
     ft_c = [send(feat_s, feat_r.at[y], dev_y(k)) for k in (2, 1, 3)]
     feat_r[y] = feat_s[...]
-    for ab in range(2):
-        side_add(ab, 0)
-        side2[ab] = second(side_part, side1, ab)
-
-    def total2(own2, land2, ab, q):
-        value = own2[ab, q]
-        for k in range(3):
-            value = value + land2[ab, k, q].astype(F32)
-        return value
-
-    x3 = []
-    for ab in range(2):
-        for w in main2[ab]:
-            w.wait_recv()
-        send3[ab] = total2(mown2, mland2, ab, 1 - xl).astype(BF16)
-        x3.append(send(send3.at[ab], land3.at[ab], xlo))
+
     wx_c[1].wait_recv()
     wc_c.append(send(hk.at[:, :, :, lanes], hk.at[:, :, :, lanes], other))
 
-    for w in ft_c:
-        w.wait_recv()
-    for q in range(4):
-        fwide[OWN * q : OWN * q + OWN, :] = unpack(feat_r[q])
-    feats = fwide[...].astype(BF16)
-    wc_c[1].wait_recv()
-    pred[...] = dot_nt(feats, hk[...].reshape(768, 1024))
     for ab in range(2):
         s = slice(384 * ab, 384 * ab + 384)
         for w in side2[ab]:
             w.wait_recv()
-        tsum[MAIN:160, s] = total2(sown2, sland2, ab, 0)
+        value = sown2[ab]
+        for k in range(3):
+            value = value + sland2[ab, k].astype(F32)
+        tsum[MAIN:160, s] = value
         x3[ab].wait_recv()
-        tsum[0:MAIN, s] = total2(mown2, mland2, ab, xl) + land3[ab].astype(F32)
+        tsum[0:MAIN, s] = main_total(ab, xl) + land3[ab].astype(F32)
 
     teach = tsum[...]
     mean_own = jnp.mean(teach, axis=-1, keepdims=True)
@@ -402,6 +409,14 @@
     tpad[0:160, :] = jnp.where(lane == 0, mean_own, jnp.where(lane == 1, m2_own, 0.0))
     stat[0] = tpad[...].T[0:8, :]
     sc = [send(stat.at[0], stat.at[k], dev_y(k)) for k in (2, 1, 3)]
+
+    for w in ft_c:
+        w.wait_recv()
+    for q in range(4):
+        fwide[OWN * q : OWN * q + OWN, :] = unpack(feat_r[q])
+    feats = fwide[...].astype(BF16)
+    wc_c[1].wait_recv()
+    pred[...] = dot_nt(feats, hk[...].reshape(768, 1024))
     for w in sc:
         w.wait_recv()
     means = [stat[k, 0:1, :] for k in range(4)]
@@ -461,6 +476,8 @@
 
     hc_c = core_out(hx, hcr)
 
+    hzc = z_out(hx, hcr, hy, hyo, hzr, hc_c)
+
     gsum = fg[y]
     for w in fg_c:
         w.wait_recv()
@@ -473,8 +490,6 @@
     sg_s[...] = pack(istd_v[:, 0:1] * (weighted - first - nrm * second))
     sg_c = [send(sg_s, sg_r.at[y], dev_y(k)) for k in (2, 1, 3)]
     sg_r[y] = sg_s[...]
-
-    hzc = z_out(hx, hcr, hy, hyo, hzr, hc_c)
 
     for w in sg_c:
         w.wait_recv()
@@ -558,16 +573,15 @@
             v(3, 2, *tail), v(2, *tail), v(4, *tail),
         ]
 
-    def ring_bufs(rows, n, r):
-        return [
-            v(2, 3, 4, rows, 384), v(2, 4, rows, 384, dtype=F32), v(2, 2, 4, rows, 384), v(2, 2, 4, rows, 384),
-            v(2, 3, n, r, 384), v(2, n, r, 384, dtype=F32), v(2, 3, n, r, 384),
-        ]
+    def ring_bufs(rows):
+        return [v(2, 3, 4, rows, 384), v(2, 4, rows, 384, dtype=F32), v(2, 2, 4, rows, 384), v(2, 2, 4, rows, 384)]
 
     scratch = [
         v(4, 2, MAIN, 768), v(2, 4, SIDE, 768), v(4, 768, 384), v(768, 1536),
-        *ring_bufs(2 * MAIN, 2, MAIN),
-        *ring_bufs(SIDE, 1, SIDE),
+        *ring_bufs(2 * MAIN),
+        v(2, 3, 2, MAIN, 384), v(2, 2, MAIN, 384, dtype=F32), v(2, 2, 2, MAIN, 384), v(2, 2, 2, MAIN, 384),
+        *ring_bufs(SIDE),
+        v(2, 3, SIDE, 384), v(2, SIDE, 384, dtype=F32), v(2, 3, SIDE, 384),
         v(2, 4, 4, SIDE, 384), v(2, 4, 4, SIDE, 384), v(2, 4, 4, SIDE, 384, dtype=F32),
         v(2, MAIN, 384), v(2, MAIN, 384),
         v(160, 768, dtype=F32),

time: 95 us -> 92.3 us (0.972)
  Pallas kernels: 94.2 us -> 91.6 us
    pallas_call x1, Pallas kernels: 92.3 us -> 89.6 us  [per_device(): pl.pallas_call(kernel, out_shape=(jax.ShapeDtypeStruct((96, 1024), F32),...]
where the time goes in v3:
time: 92.3 us; the launch traced here: 92.2 us
  Pallas kernels  91.6 us (99%)
    pallas_call x1, Pallas kernels, per_device(): pl.pallas_call(kernel, out_shape=(jax.ShapeDtypeStruct((96, 1024), F32),...  89.6 us
    pallas_call x1, Pallas kernels, per_device(): pl.pallas_call(emit, out_shape=(jax.ShapeDtypeStruct((96, 1024), F32), ja...  1.92 us

profile of v3, /device:TPU:1, one launch (start us, length us, event | category | flops | bytes accessed | tf_op | source)
XLA Modules:
  0.0 92.2 jit_solution(10534573391273956563)
XLA Ops:
  0.6 89.6 %shard_map.95 = (f32[96,1024]{1,0:T(8,128)}, f32[2,32,1024]{2,1,0:T(8,128)}) custom-call(bf16[8,160,768]{2,1,0:T(8,128)(2,1)} %bitcast.5, bf16[768,3072]{1,0:T(8,128)(2,1)} %down.1, f32[2,4,1,384]{3,2,1,0:T(1,128)} %bitcast.8, bf16[40,1024]{1,0:T(8,128)(2,1)} %stream_in.1, bf16[2,40,1024]{2,1,0:T(8,128)(2,1)} %ctx.1, bf16[2,32,1024]{2,1,0:T(8,128)(2,1)} %pw.1, ...), custom_call_target="tpu_custom_call" | custom-call | flops 6000000000 | bytes 8000000 | tf_op jit(solution)/shard_map/pallas_call | solution.py:602
  90.3 1.9 %shard_map.96 = (f32[96,1024]{1,0:T(8,128)}, f32[2,32,1024]{2,1,0:T(8,128)}) custom-call(f32[96,1024]{1,0:T(8,128)} %get-tuple-element.6.hg_in, f32[2,32,1024]{2,1,0:T(8,128)} %get-tuple-element.7.pg_in), custom_call_target="tpu_custom_call" | custom-call | tf_op jit(solution)/shard_map/pallas_call | solution.py:625

commit v4 on v3

--- a/solution.py
+++ b/solution.py
@@ -204,23 +204,6 @@
     main2 = [Ring(dev_z, 0, 2, msend2, mrly2, mland2), Ring(dev_y, 1, 2, msend2, mrly2, mland2)]
     side1 = [Ring(dev_y, 0, 4, ssend1, srly1, sland1), Ring(dev_z, 1, 4, ssend1, srly1, sland1)]
 
-    for i in range(3):
-        loads[i].wait()
-    main_product(0, 2)
-    pl.semaphore_wait(barrier, 14)
-    main1[0].relay_out()
-    for i in range(3, 6):
-        loads[i].wait()
-    main_product(1, 2)
-    main1[1].relay_out()
-    xc = [[None] * 4, [None] * 4]
-
-    def x_first(ab, k):
-        xc[ab][k] = send(xs.at[ab, k], xr.at[ab, k], xlo)
-
-    side_product_y(2, 1 - xl, xs)
-    x_first(0, 2)
-
     strm_s[...] = pack(stream_in[...].astype(F32))
     for q in range(4):
         parts = [
@@ -229,6 +212,7 @@
             for half in range(2)
         ]
         ctx_s[q] = jnp.concatenate(parts, axis=0).astype(BF16)
+    pl.semaphore_wait(barrier, 14)
     strm_self = jnp.logical_and(y == z, z == y)
     strm_to = pltpu.make_async_remote_copy(
         src_ref=strm_s, dst_ref=strm_r, send_sem=usem.at[8], recv_sem=usem.at[9],
@@ -262,9 +246,27 @@
 
     loads[6].wait()
     wz_c = [send(wk.at[:, xl, z, :, lanes], wk.at[:, xl, z, :, lanes], dev_z(k)) for k in (2, 1, 3)]
+    for i in range(3):
+        loads[i].wait()
+    main_product(0, 2)
+    main1[0].relay_out()
+    for i in range(3, 6):
+        loads[i].wait()
+    main_product(1, 2)
+    main1[1].relay_out()
+    loads[7].wait()
+    hz_c = [send(hk.at[xl, z, :, lanes], hk.at[xl, z, :, lanes], dev_z(k)) for k in (2, 1, 3)]
+    xc = [[None] * 4, [None] * 4]
+
+    def x_first(ab, k):
+        xc[ab][k] = send(xs.at[ab, k], xr.at[ab, k], xlo)
+
+    side_product_y(2, 1 - xl, xs)
+    x_first(0, 2)
+
     side_product_z(1 - xl, xs)
     x_first(1, 2)
-    for i in range(7, 11):
+    for i in range(8, 11):
         loads[i].wait()
     for ab in range(2):
         for k in (1, 3):
@@ -274,6 +276,9 @@
         side_product_y(k, 1 - xl, xs)
         x_first(0, k)
         x_first(1, k)
+    for w in wz_c:
+        w.wait_recv()
+    wx_c = [send(wk.at[:, xl, :, :, lanes], wk.at[:, xl, :, :, lanes], xhi)]
     main_product(0, 0)
     main_product(1, 0)
     for k in (2, 1, 3, 0):
@@ -281,7 +286,6 @@
     side_product_z(xl, xown)
     for ab in range(2):
         main1[ab].relay_on()
-    hz_c = [send(hk.at[xl, z, :, lanes], hk.at[xl, z, :, lanes], dev_z(k)) for k in (2, 1, 3)]
 
     def side_add(ab, k):
         xc[ab][k].wait_recv()
@@ -294,13 +298,6 @@
     for ab in range(2):
         side_add(ab, 2)
         side1[ab].relay_out()
-    for w in wz_c:
-        w.wait_recv()
-    wx_c = [send(wk.at[:, xl, :, :, lanes], wk.at[:, xl, :, :, lanes], xhi)]
-    for ab in range(2):
-        side_add(ab, 1)
-        side1[ab].direct_out(1)
-
     for j in range(4):
         pltpu.make_async_remote_copy(
             src_ref=ctx_s.at[j], dst_ref=ctx_r.at[j], send_sem=usem.at[j], recv_sem=tsem.at[j],
@@ -316,6 +313,13 @@
     for k in (2, 1, 3):
         st_s[k - 1] = pack(fg[(y + k) % 4])
     st_c = [send(st_s.at[k - 1], st_r.at[k - 1], dev_y(k)) for k in (2, 1, 3)]
+    for w in hz_c:
+        w.wait_recv()
+    wx_c.append(send(hk.at[xl, :, :, lanes], hk.at[xl, :, :, lanes], xhi))
+    for ab in range(2):
+        side_add(ab, 1)
+        side1[ab].direct_out(1)
+
 
     def total1(own1, land1, ab, k):
         q = ((z if ab == 0 else y) + k) % 4
@@ -355,23 +359,6 @@
     side1[1].direct_out(3)
     side1[1].relay_on()
     main_second(1)
-    for w in hz_c:
-        w.wait_recv()
-    wx_c.append(send(hk.at[xl, :, :, lanes], hk.at[xl, :, :, lanes], xhi))
-    main2[0].relay_on()
-    main2[1].relay_on()
-    side2 = []
-    for ab in range(2):
-        side_add(ab, 0)
-        side2.append(side_second(ab))
-    def main_total(ab, q):
-        return mown2[ab, q] + mland2[ab, 0, q].astype(F32) + mland2[ab, 1, q].astype(F32)
-
-    x3 = []
-    for ab in range(2):
-        main2[ab].finish()
-        send3[ab] = main_total(ab, 1 - xl).astype(BF16)
-        x3.append(send(send3.at[ab], land3.at[ab], xlo))
     strm_to.wait_recv()
     stream = unpack(strm_r[...]) + fg[y]
     for w in st_c:
@@ -386,9 +373,23 @@
     feat_s[...] = pack(normed * sgain[...])
     ft_c = [send(feat_s, feat_r.at[y], dev_y(k)) for k in (2, 1, 3)]
     feat_r[y] = feat_s[...]
-
     wx_c[1].wait_recv()
     wc_c.append(send(hk.at[:, :, :, lanes], hk.at[:, :, :, lanes], other))
+    main2[0].relay_on()
+    main2[1].relay_on()
+    side2 = []
+    for ab in range(2):
+        side_add(ab, 0)
+        side2.append(side_second(ab))
+    def main_total(ab, q):
+        return mown2[ab, q] + mland2[ab, 0, q].astype(F32) + mland2[ab, 1, q].astype(F32)
+
+    x3 = []
+    for ab in range(2):
+        main2[ab].finish()
+        send3[ab] = main_total(ab, 1 - xl).astype(BF16)
+        x3.append(send(send3.at[ab], land3.at[ab], xlo))
+
 
     for ab in range(2):
         s = slice(384 * ab, 384 * ab + 384)

time: 92.3 us -> 92 us (level)
  no operation moved by 1% of the time
where the time goes in v4:
time: 92 us; the launch traced here: 91.8 us
  Pallas kernels  91.2 us (99%)
    pallas_call x1, Pallas kernels, per_device(): pl.pallas_call(kernel, out_shape=(jax.ShapeDtypeStruct((96, 1024), F32),...  89.3 us
    pallas_call x1, Pallas kernels, per_device(): pl.pallas_call(emit, out_shape=(jax.ShapeDtypeStruct((96, 1024), F32), ja...  1.92 us

profile of v4, /device:TPU:1, one launch (start us, length us, event | category | flops | bytes accessed | tf_op | source)
XLA Modules:
  0.0 91.8 jit_solution(12123215914910705553)
XLA Ops:
  0.6 89.3 %shard_map.95 = (f32[96,1024]{1,0:T(8,128)}, f32[2,32,1024]{2,1,0:T(8,128)}) custom-call(bf16[8,160,768]{2,1,0:T(8,128)(2,1)} %bitcast.5, bf16[768,3072]{1,0:T(8,128)(2,1)} %down.1, f32[2,4,1,384]{3,2,1,0:T(1,128)} %bitcast.8, bf16[40,1024]{1,0:T(8,128)(2,1)} %stream_in.1, bf16[2,40,1024]{2,1,0:T(8,128)(2,1)} %ctx.1, bf16[2,32,1024]{2,1,0:T(8,128)(2,1)} %pw.1, ...), custom_call_target="tpu_custom_call" | custom-call | flops 6000000000 | bytes 8000000 | tf_op jit(solution)/shard_map/pallas_call | solution.py:603
  89.9 1.9 %shard_map.96 = (f32[96,1024]{1,0:T(8,128)}, f32[2,32,1024]{2,1,0:T(8,128)}) custom-call(f32[96,1024]{1,0:T(8,128)} %get-tuple-element.6.hg_in, f32[2,32,1024]{2,1,0:T(8,128)} %get-tuple-element.7.pg_in), custom_call_target="tpu_custom_call" | custom-call | tf_op jit(solution)/shard_map/pallas_call | solution.py:626

commit v5 on v4

--- a/solution.py
+++ b/solution.py
@@ -515,7 +515,8 @@
     for layer in range(2):
         px, pcr, py, pyo, pzr, pz, pxr = pbufs[layer]
         pzc.append(z_out(px, pcr, py, pyo, pzr, pc_c[layer]))
-    hxc = x_out(hyo, hzr, hz, hxr, hzc)
+        if layer == 0:
+            hxc = x_out(hyo, hzr, hz, hxr, hzc)
     pxc = []
     for layer in range(2):
         px, pcr, py, pyo, pzr, pz, pxr = pbufs[layer]

time: 92 us -> 92.3 us (level)
  no operation moved by 1% of the time
where the time goes in v5:
time: 92.3 us; the launch traced here: 92.1 us
  Pallas kernels  91.5 us (99%)
    pallas_call x1, Pallas kernels, per_device(): pl.pallas_call(kernel, out_shape=(jax.ShapeDtypeStruct((96, 1024), F32),...  89.6 us
    pallas_call x1, Pallas kernels, per_device(): pl.pallas_call(emit, out_shape=(jax.ShapeDtypeStruct((96, 1024), F32), ja...  1.92 us

profile of v5, /device:TPU:1, one launch (start us, length us, event | category | flops | bytes accessed | tf_op | source)
XLA Modules:
  0.0 92.1 jit_solution(15345887573261205635)
XLA Ops:
  0.6 89.6 %shard_map.95 = (f32[96,1024]{1,0:T(8,128)}, f32[2,32,1024]{2,1,0:T(8,128)}) custom-call(bf16[8,160,768]{2,1,0:T(8,128)(2,1)} %bitcast.5, bf16[768,3072]{1,0:T(8,128)(2,1)} %down.1, f32[2,4,1,384]{3,2,1,0:T(1,128)} %bitcast.8, bf16[40,1024]{1,0:T(8,128)(2,1)} %stream_in.1, bf16[2,40,1024]{2,1,0:T(8,128)(2,1)} %ctx.1, bf16[2,32,1024]{2,1,0:T(8,128)(2,1)} %pw.1, ...), custom_call_target="tpu_custom_call" | custom-call | flops 6000000000 | bytes 8000000 | tf_op jit(solution)/shard_map/pallas_call | solution.py:604
  90.2 1.9 %shard_map.96 = (f32[96,1024]{1,0:T(8,128)}, f32[2,32,1024]{2,1,0:T(8,128)}) custom-call(f32[96,1024]{1,0:T(8,128)} %get-tuple-element.6.hg_in, f32[2,32,1024]{2,1,0:T(8,128)} %get-tuple-element.7.pg_in), custom_call_target="tpu_custom_call" | custom-call | tf_op jit(solution)/shard_map/pallas_call | solution.py:627
